TPU v7x, 256 devices: a whole 4x4x8 slice. The times are simulated.
256 devices in a mesh: dp: 8 (over y, core), expert: 32 (over z, x).
Axes of the slice: x: 4, y: 4, z: 8, core: 2. Of those that a mesh axis runs over, the one named last changes fastest.
Arguments:
- tokens: bfloat16 [12288, 2048], P(('dp', 'expert')), may hold values from -6 to 6
- expert_ids: int32 [12288, 8], P(('dp', 'expert')), may hold values from 0 to 31, all different within a row; in each aligned block of 48 rows (0 to 47, 48 to 95, ...) at most 18 rows name the same one
- gate_weights: float32 [12288, 8], P(('dp', 'expert')), may hold values from 0.05 to 1
- up_weight: bfloat16 [32, 2048, 768], P('expert'), may hold values from -0.125 to 0.125
- down_weight: bfloat16 [32, 768, 2048], P('expert'), may hold values from -0.21875 to 0.21875
- out_grad: bfloat16 [12288, 2048], P(('dp', 'expert')), may hold values from -0.59765625 to 0.59765625
Outputs:
- mixed: bfloat16 [12288, 2048], P(('dp', 'expert'))
- grad_tokens: bfloat16 [12288, 2048], P(('dp', 'expert'))
- grad_up: bfloat16 [32, 2048, 768], P('expert')
- grad_down: bfloat16 [32, 768, 2048], P('expert')
Inputs may be any that keep to these rules, and one draw needn't show every extreme that they name: `expert_ids`: the 8 experts of a token are distinct. Among the 48 tokens of one device at most 18 name any one expert, and in every draw some device has 18 tokens naming one expert.
All inputs are finite; a program needn't handle non-finite values.
Results may differ from a plain program's by a relative error of at most 0.017.
Values may be sent and summed in bfloat16 or wider, within the bound.
A program may use at most 128 MiB of HBM per device.

v0:
```python
import jax
import jax.numpy as jnp
from jax import lax
from jax.sharding import PartitionSpec as P


def silu_slope(pre_act):
    sigmoid = jax.nn.sigmoid(pre_act)
    return sigmoid * (1.0 + pre_act * (1.0 - sigmoid))


def contract(left, right, left_dim, right_dim):
    return lax.dot_general(
        left, right, (((left_dim,), (right_dim,)), ((), ())), preferred_element_type=jnp.float32
    )


def forward_block(rows_x, up_local, down_local):
    pre_act = jnp.dot(rows_x, up_local, preferred_element_type=jnp.float32)
    hidden = jax.nn.silu(pre_act).astype(jnp.bfloat16)
    expert_out = jnp.dot(hidden, down_local, preferred_element_type=jnp.float32).astype(
        jnp.bfloat16
    )
    return (pre_act, hidden, expert_out)


def backward_block(rows_dy, pre_act, up_local, down_local):
    linear = contract(rows_dy, down_local, 1, 1)
    pre_grad = (linear * silu_slope(pre_act)).astype(jnp.bfloat16)
    grad_rows = contract(pre_grad, up_local, 1, 1).astype(jnp.bfloat16)
    return (pre_grad, grad_rows)


def shards(tokens, expert_ids, gate_weights, up_weight, down_weight, out_grad):
    experts = lax.axis_size("expert")
    tok_count, top_count = expert_ids.shape
    slot_rows = tok_count * top_count * 3 // (2 * experts)
    recv_rows = experts * slot_rows
    model_width = tokens.shape[1]
    up_local = up_weight[0]
    down_local = down_weight[0]
    matches = (
        expert_ids[:, :, None] == jnp.arange(experts, dtype=jnp.int32)[None, None, :]
    ).astype(jnp.int32)
    hit_table = jnp.sum(matches, axis=1)
    before = jnp.cumsum(hit_table, axis=0) - hit_table
    slot_place = jnp.sum(matches * before[:, None, :], axis=2)
    target = (expert_ids * slot_rows + slot_place).reshape(-1)
    source = jnp.repeat(
        jnp.arange(tok_count, dtype=jnp.int32), top_count, total_repeat_length=tok_count * top_count
    )
    counts = jnp.sum(hit_table, axis=0).astype(jnp.bfloat16).reshape(experts, 1)
    send_x = jnp.zeros((recv_rows, model_width), jnp.bfloat16).at[target].set(tokens[source])
    send_x = send_x.reshape(experts, slot_rows, model_width)
    scaled = (gate_weights.reshape(-1)[:, None] * out_grad[source].astype(jnp.float32)).astype(
        jnp.bfloat16
    )
    send_dy = jnp.zeros((recv_rows, model_width), jnp.bfloat16).at[target].set(scaled)
    send_dy = send_dy.reshape(experts, slot_rows, model_width)
    got_x, got_counts = (
        lax.all_to_all(send_x, "expert", split_axis=0, concat_axis=0, tiled=True),
        lax.all_to_all(counts, "expert", split_axis=0, concat_axis=0, tiled=True),
    )
    x_rows = got_x.reshape(recv_rows, model_width)
    pre_rows, hidden_rows, out_rows = forward_block(x_rows, up_local, down_local)
    back_out = lax.all_to_all(
        out_rows.reshape(experts, slot_rows, model_width),
        "expert",
        split_axis=0,
        concat_axis=0,
        tiled=True,
    )
    gathered = back_out.reshape(recv_rows, model_width)[target].reshape(
        tok_count, top_count, model_width
    )
    mixed = jnp.sum(gate_weights[:, :, None] * gathered.astype(jnp.float32), axis=1).astype(
        jnp.bfloat16
    )
    got_dy = lax.all_to_all(send_dy, "expert", split_axis=0, concat_axis=0, tiled=True)
    dy_rows = got_dy.reshape(recv_rows, model_width)
    down_grad = contract(hidden_rows, dy_rows, 0, 0)
    pre_grad, grad_rows = backward_block(dy_rows, pre_rows, up_local, down_local)
    up_grad = contract(x_rows, pre_grad, 0, 0)
    back_grad = lax.all_to_all(
        grad_rows.reshape(experts, slot_rows, model_width),
        "expert",
        split_axis=0,
        concat_axis=0,
        tiled=True,
    )
    grad_pairs = back_grad.reshape(recv_rows, model_width)[target].reshape(
        tok_count, top_count, model_width
    )
    grad_tokens = jnp.sum(grad_pairs.astype(jnp.float32), axis=1).astype(jnp.bfloat16)
    up_sum, down_sum = (
        lax.psum(up_grad.astype(jnp.bfloat16), "dp").astype(jnp.float32),
        lax.psum(down_grad.astype(jnp.bfloat16), "dp").astype(jnp.float32),
    )
    return (
        mixed,
        grad_tokens,
        up_sum.astype(jnp.bfloat16)[None],
        down_sum.astype(jnp.bfloat16)[None],
    )


def solution(mesh):
    return jax.shard_map(
        shards,
        mesh=mesh,
        in_specs=(
            P(("dp", "expert"), None),
            P(("dp", "expert"), None),
            P(("dp", "expert"), None),
            P("expert", None, None),
            P("expert", None, None),
            P(("dp", "expert"), None),
        ),
        out_specs=(
            P(("dp", "expert"), None),
            P(("dp", "expert"), None),
            P("expert", None, None),
            P("expert", None, None),
        ),
        check_vma=False,
    )
```

profile of v0, /device:TPU:1, one launch (start us, length us, event | category | flops | bytes accessed | tf_op | source)
XLA Modules:
  0.0 419.1 jit_solution(2827004243275815858)
XLA Ops:
  10.9 4.5 %fusion.27 = (s32[384]{0:T(512)S(1)}, s32[384,1]{0,1:T(1,128)S(1)}) fusion(s32[]{:T(128)} %bitcast.41, s32[]{:T(128)} %bitcast.42, s32[]{:T(128)} %bitcast.43, s32[]{:T(128)} %bitcast.44, s32[]{:T(128)} %bitcast.45, s32[]{:T(128)} %bitcast.47, s32[]{:T(128)} %bitcast.46, s32[1,1,3,128]{3,2,1,0:T(4,128)S(1)} %get-tuple-element.62, ...), kind=kLoop, calls=%fused_computation.95 | loop fusion | flops 5376 | bytes 6172 | tf_op jit(solution)/shard_map/jit(_take)/gather | solution.py:49
  15.6 25.6 %select_select_fusion = s32[384]{0:T(512)S(1)} fusion(pred[384]{0:T(512)(128)(4,1)S(1)} %get-tuple-element.55, pred[384]{0:T(512)(128)(4,1)S(1)} %get-tuple-element.54, pred[384]{0:T(512)(128)(4,1)S(1)} %get-tuple-element.56, pred[384]{0:T(512)(128)(4,1)S(1)} %get-tuple-element.53, pred[384]{0:T(512)(128)(4,1)S(1)} %get-tuple-element.52, ...), kind=kLoop, calls=%fused_computation.94 | loop fusion | flops 15744 | bytes 18980 | tf_op jit(solution)/shard_map/jit(_take)/gather | solution.py:49
  43.0 10.9 %scatter_custom_fusion = bf16[576,2048]{1,0:T(8,128)(2,1)} fusion(s32[384]{0:T(512)S(1)} %fusion.28, bf16[48,2048]{1,0:T(8,128)(2,1)} %param.8, s32[1024]{0:T(1024)S(1)} %pad_clamp_fusion.1, bf16[]{:T(256)} %constant.95.clone.1), kind=kCustom, calls=%fused_computation.28 | custom fusion | bytes 2359808 | tf_op jit(solution)/shard_map/scatter | solution.py:53
  53.9 4.3 %reshape.186 = bf16[32,18,2048]{2,1,0:T(8,128)(2,1)} reshape(bf16[576,2048]{1,0:T(8,128)(2,1)} %scatter_custom_fusion) | data formatting | bytes 4718592 | tf_op jit(solution)/shard_map/reshape | solution.py:54
  58.2 12.3 %all-to-all-start = ((bf16[32,18,2048]{2,1,0:T(8,128)(2,1)}), bf16[32,18,2048]{2,1,0:T(8,128)(2,1)}, u32[]{:S(2)}, u32[]{:S(2)}) async-start(bf16[32,18,2048]{2,1,0:T(8,128)(2,1)} %reshape.186), calls=%async_computation | async-start | bytes 6291456 | tf_op jit(solution)/shard_map/all_to_all | solution.py:61
  70.7 9.6 %scatter_custom_fusion.1 = bf16[576,2048]{1,0:T(8,128)(2,1)} fusion(s32[384]{0:T(512)S(1)} %fusion.28, f32[384]{0:T(512)S(1)} %mul.52, bf16[]{:T(256)} %constant.95.clone.1, bf16[48,2048]{1,0:T(8,128)(2,1)S(1)} %copy-done.6, s32[1024]{0:T(1024)S(1)} %pad_clamp_fusion.1), kind=kCustom, calls=%fused_computation.26 | custom fusion | flops 2359296 | bytes 2562050 | tf_op jit(solution)/shard_map/scatter | solution.py:58
  80.3 4.3 %reshape.190 = bf16[32,18,2048]{2,1,0:T(8,128)(2,1)} reshape(bf16[576,2048]{1,0:T(8,128)(2,1)} %scatter_custom_fusion.1) | data formatting | bytes 4718592 | tf_op jit(solution)/shard_map/reshape | solution.py:59
  84.6 56.4 %all-to-all-done = bf16[32,18,2048]{2,1,0:T(8,128)(2,1)} async-done(((bf16[32,18,2048]{2,1,0:T(8,128)(2,1)}), bf16[32,18,2048]{2,1,0:T(8,128)(2,1)}, u32[]{:S(2)}, u32[]{:S(2)}) %all-to-all-start) | async-done | bytes 2359328 | tf_op jit(solution)/shard_map/all_to_all | solution.py:61
  141.0 7.9 %all-to-all-start.2 = ((bf16[32,18,2048]{2,1,0:T(8,128)(2,1)}), bf16[32,18,2048]{2,1,0:T(8,128)(2,1)}, u32[]{:S(2)}, u32[]{:S(2)}) async-start(bf16[32,18,2048]{2,1,0:T(8,128)(2,1)} %reshape.190), calls=%async_computation.2 | async-start | bytes 6291456 | tf_op jit(solution)/shard_map/all_to_all | solution.py:79
  148.9 4.4 %reshape.187 = bf16[576,2048]{1,0:T(8,128)(2,1)} reshape(bf16[32,18,2048]{2,1,0:T(8,128)(2,1)} %all-to-all-done) | data formatting | bytes 4718592 | tf_op jit(solution)/shard_map/reshape | solution.py:64
  153.3 4.6 %fusion.7 = f32[576,768]{1,0:T(8,128)S(1)} fusion(bf16[576,2048]{1,0:T(8,128)(2,1)} %reshape.187, bf16[1,2048,768]{2,1,0:T(8,128)(2,1)} %param.11), kind=kOutput, calls=%fused_computation.16 | convolution fusion | flops 1811939328 | bytes 7274496 | tf_op jit(solution)/shard_map/dot_general | solution.py:19
  159.1 3.5 fusion.12
  162.5 4.3 %reshape.188 = bf16[32,18,2048]{2,1,0:T(8,128)(2,1)} reshape(bf16[576,2048]{1,0:T(8,128)(2,1)} %fusion.12) | data formatting | bytes 4718592 | tf_op jit(solution)/shard_map/reshape | solution.py:67
  166.8 52.9 %all-to-all-done.2 = bf16[32,18,2048]{2,1,0:T(8,128)(2,1)} async-done(((bf16[32,18,2048]{2,1,0:T(8,128)(2,1)}), bf16[32,18,2048]{2,1,0:T(8,128)(2,1)}, u32[]{:S(2)}, u32[]{:S(2)}) %all-to-all-start.2) | async-done | bytes 2359328 | tf_op jit(solution)/shard_map/all_to_all | solution.py:79
  219.7 6.6 %all-to-all-start.1 = ((bf16[32,18,2048]{2,1,0:T(8,128)(2,1)}), bf16[32,18,2048]{2,1,0:T(8,128)(2,1)}, u32[]{:S(2)}, u32[]{:S(2)}) async-start(bf16[32,18,2048]{2,1,0:T(8,128)(2,1)} %reshape.188), calls=%async_computation.1 | async-start | bytes 6291456 | tf_op jit(solution)/shard_map/all_to_all | solution.py:66
  226.4 4.4 %reshape.191 = bf16[576,2048]{1,0:T(8,128)(2,1)} reshape(bf16[32,18,2048]{2,1,0:T(8,128)(2,1)} %all-to-all-done.2) | data formatting | bytes 4718592 | tf_op jit(solution)/shard_map/reshape | solution.py:80
  230.8 4.6 %multiply_convert_fusion.1 = bf16[576,768]{1,0:T(8,128)(2,1)S(1)} fusion(f32[576,768]{1,0:T(8,128)} %copy-done.9, bf16[576,2048]{1,0:T(8,128)(2,1)} %reshape.191, bf16[1,768,2048]{2,1,0:T(8,128)(2,1)S(1)} %copy-done), kind=kOutput, calls=%fused_computation.23 | convolution fusion | flops 1815920640 | bytes 8159232 | tf_op jit(solution)/shard_map/dot_general | solution.py:13
  240.8 55.6 %all-to-all-done.1 = bf16[32,18,2048]{2,1,0:T(8,128)(2,1)} async-done(((bf16[32,18,2048]{2,1,0:T(8,128)(2,1)}), bf16[32,18,2048]{2,1,0:T(8,128)(2,1)}, u32[]{:S(2)}, u32[]{:S(2)}) %all-to-all-start.1) | async-done | bytes 2359328 | tf_op jit(solution)/shard_map/all_to_all | solution.py:66
  296.4 6.8 %all-to-all-start.3 = ((bf16[32,18,2048]{2,1,0:T(8,128)(2,1)}), bf16[32,18,2048]{2,1,0:T(8,128)(2,1)}, u32[]{:S(2)}, u32[]{:S(2)}) async-start(bf16[32,18,2048]{2,1,0:T(8,128)(2,1)} %reshape.192), calls=%async_computation.3 | async-start | bytes 6291456 | tf_op jit(solution)/shard_map/all_to_all | solution.py:84
  303.5 5.4 %fusion.15 = bf16[1,2048,768]{2,1,0:T(8,128)(2,1)} fusion(bf16[576,2048]{1,0:T(8,128)(2,1)S(1)} %copy-done.4, bf16[576,768]{1,0:T(8,128)(2,1)} %copy-done.11), kind=kOutput, calls=%fused_computation.21 | convolution fusion | flops 1813512192 | bytes 6389760 | tf_op jit(solution)/shard_map/dot_general | solution.py:13
  308.9 4.1 fusion.16
  319.1 53.4 %all-to-all-done.3 = bf16[32,18,2048]{2,1,0:T(8,128)(2,1)} async-done(((bf16[32,18,2048]{2,1,0:T(8,128)(2,1)}), bf16[32,18,2048]{2,1,0:T(8,128)(2,1)}, u32[]{:S(2)}, u32[]{:S(2)}) %all-to-all-start.3) | async-done | bytes 2359328 | tf_op jit(solution)/shard_map/all_to_all | solution.py:84
  384.1 22.6 %all-reduce.3.cloned.1.call-done = (bf16[1,2048,768]{2,1,0:T(8,128)(2,1)}, bf16[1,768,2048]{2,1,0:T(8,128)(2,1)}) async-done(((bf16[1,2048,768]{2,1,0:T(8,128)(2,1)}, bf16[1,768,2048]{2,1,0:T(8,128)(2,1)}), (bf16[1,2048,768]{2,1,0:T(8,128)(2,1)}, bf16[1,768,2048]{2,1,0:T(8,128)(2,1)})) %all-reduce.3.cloned.1.call-update) | async-done | bytes 6291472 | tf_op jit(solution)/shard_map/psum | solution.py:96
  406.7 3.9 copy.30
  (57 shorter events, 32.2 us)
Async XLA Ops:
  7.2 151.9 %copy-start = (bf16[1,768,2048]{2,1,0:T(8,128)(2,1)S(1)}, bf16[1,768,2048]{2,1,0:T(8,128)(2,1)}, u32[]{:S(2)}) copy-start(bf16[1,768,2048]{2,1,0:T(8,128)(2,1)} %param.12) | copy-start | bytes 9437188
  58.2 12.3 %copy-start.7 = (f32[48,8]{0,1:T(8,128)S(1)}, f32[48,8]{0,1:T(8,128)}, u32[]{:S(2)}) copy-start(f32[48,8]{0,1:T(8,128)} %param.10) | copy-start | bytes 4612
  58.2 12.5 %copy-start.6 = (bf16[48,2048]{1,0:T(8,128)(2,1)S(1)}, bf16[48,2048]{1,0:T(8,128)(2,1)}, u32[]{:S(2)}) copy-start(bf16[48,2048]{1,0:T(8,128)(2,1)} %param.13) | copy-start | bytes 589828
  58.2 82.8 %all-to-all-start = ((bf16[32,18,2048]{2,1,0:T(8,128)(2,1)}), bf16[32,18,2048]{2,1,0:T(8,128)(2,1)}, u32[]{:S(2)}, u32[]{:S(2)}) async-start(bf16[32,18,2048]{2,1,0:T(8,128)(2,1)} %reshape.186), calls=%async_computation | async-start | bytes 6291456 | tf_op jit(solution)/shard_map/all_to_all | solution.py:61
  141.0 78.7 %all-to-all-start.2 = ((bf16[32,18,2048]{2,1,0:T(8,128)(2,1)}), bf16[32,18,2048]{2,1,0:T(8,128)(2,1)}, u32[]{:S(2)}, u32[]{:S(2)}) async-start(bf16[32,18,2048]{2,1,0:T(8,128)(2,1)} %reshape.190), calls=%async_computation.2 | async-start | bytes 6291456 | tf_op jit(solution)/shard_map/all_to_all | solution.py:79
  157.9 1.2 copy-start.9
  219.7 76.7 %all-to-all-start.1 = ((bf16[32,18,2048]{2,1,0:T(8,128)(2,1)}), bf16[32,18,2048]{2,1,0:T(8,128)(2,1)}, u32[]{:S(2)}, u32[]{:S(2)}) async-start(bf16[32,18,2048]{2,1,0:T(8,128)(2,1)} %reshape.188), calls=%async_computation.1 | async-start | bytes 6291456 | tf_op jit(solution)/shard_map/all_to_all | solution.py:66
  230.8 5.6 %copy-start.8 = (bf16[1,2048,768]{2,1,0:T(8,128)(2,1)S(1)}, bf16[1,2048,768]{2,1,0:T(8,128)(2,1)}, u32[]{:S(2)}) copy-start(bf16[1,2048,768]{2,1,0:T(8,128)(2,1)} %param.11) | copy-start | bytes 9437188
  235.4 1.0 copy-start.11
  240.8 62.7 %copy-start.4 = (bf16[576,2048]{1,0:T(8,128)(2,1)S(1)}, bf16[576,2048]{1,0:T(8,128)(2,1)}, u32[]{:S(2)}) copy-start(bf16[576,2048]{1,0:T(8,128)(2,1)} %reshape.187) | copy-start | bytes 7077892
  296.4 76.1 %all-to-all-start.3 = ((bf16[32,18,2048]{2,1,0:T(8,128)(2,1)}), bf16[32,18,2048]{2,1,0:T(8,128)(2,1)}, u32[]{:S(2)}, u32[]{:S(2)}) async-start(bf16[32,18,2048]{2,1,0:T(8,128)(2,1)} %reshape.192), calls=%async_computation.3 | async-start | bytes 6291456 | tf_op jit(solution)/shard_map/all_to_all | solution.py:84
  303.2 103.5 %all-reduce.3.cloned.1.call-start = ((), (), s32[]{:S(2)}) async-start(), calls=%async_computation.4 | async-start | bytes 12582912 | tf_op jit(solution)/shard_map/psum | solution.py:96
  303.5 5.4 %copy-start.5 = (bf16[576,2048]{1,0:T(8,128)(2,1)S(1)}, bf16[576,2048]{1,0:T(8,128)(2,1)}, u32[]{:S(2)}) copy-start(bf16[576,2048]{1,0:T(8,128)(2,1)} %reshape.191) | copy-start | bytes 7077892
  303.5 5.4 %copy-start.10 = (f32[576,768]{1,0:T(8,128)S(1)}, f32[576,768]{1,0:T(8,128)}, u32[]{:S(2)}) copy-start(f32[576,768]{1,0:T(8,128)} %copy-done.9) | copy-start | bytes 5308420
  378.7 3.3 copy-start.2
  406.7 3.9 copy-start.3
  406.7 5.6 %copy-start.1 = (bf16[1,768,2048]{2,1,0:T(8,128)(2,1)S(1)}, bf16[1,768,2048]{2,1,0:T(8,128)(2,1)}, u32[]{:S(2)}) copy-start(bf16[1,768,2048]{2,1,0:T(8,128)(2,1)} %param.12) | copy-start | bytes 9437188
Sparse Core Ops, SparseCore 0:
  313.1 93.5 all-reduce.2
where the time goes:
time: 421 us; the launch traced here: 419 us
  waiting for transfers between devices  241 us (57%)
  local copies, waits for them, and re-layouts  57.6 us (14%)
  other arithmetic  48.4 us (11%)
  starting transfers between devices  33.9 us (8%)
  matrix products  24.1 us (6%)
  between operations  14.2 us (3%)
    all_to_all x1, waiting for transfers between devices, shards(): lax.all_to_all(send_x, 'expert', split_axis=0, concat_axis=0, tiled=True)  56.4 us
    all_to_all x1, waiting for transfers between devices, shards(): lax.all_to_all(out_rows.reshape(experts, slot_rows, model_width), 'expert...  55.6 us
    all_to_all x1, waiting for transfers between devices, shards(): lax.all_to_all(grad_rows.reshape(experts, slot_rows, model_width), 'exper...  53.4 us
    all_to_all x1, waiting for transfers between devices, shards(): lax.all_to_all(send_dy, 'expert', split_axis=0, concat_axis=0, tiled=True)  52.9 us
    gather x3, other arithmetic, shards(): jnp.repeat(jnp.arange(tok_count, dtype=jnp.int32), top_count, total_repea...  30.3 us
    psum x1, waiting for transfers between devices, shards(): lax.psum(up_grad.astype(jnp.bfloat16), 'dp').astype(jnp.float32)  22.6 us
    dot_general x4, matrix products, contract(): lax.dot_general(left, right, (((left_dim,), (right_dim,)), ((), ())), pre...  16.1 us
    all_to_all x1, starting transfers between devices, shards(): lax.all_to_all(send_x, 'expert', split_axis=0, concat_axis=0, tiled=True)  12.3 us
  transfers between devices with their start and end apart: 5, of which 5 were waited for; matrix products, arithmetic and copies ran while one was open for 17% of the time, Pallas kernels for 0%

commit v1 on v0

--- a/solution.py
+++ b/solution.py
@@ -2,6 +2,11 @@
 import jax.numpy as jnp
 from jax import lax
 from jax.sharding import PartitionSpec as P
+
+
+def _remake_rails(payload, ax_name="dp"):
+    e_now = jnp.sum(lax.all_gather(payload, ax_name), 0)
+    return e_now
 
 
 def silu_slope(pre_act):
@@ -93,7 +98,7 @@
     )
     grad_tokens = jnp.sum(grad_pairs.astype(jnp.float32), axis=1).astype(jnp.bfloat16)
     up_sum, down_sum = (
-        lax.psum(up_grad.astype(jnp.bfloat16), "dp").astype(jnp.float32),
+        _remake_rails(up_grad.astype(jnp.bfloat16)).astype(jnp.float32),
         lax.psum(down_grad.astype(jnp.bfloat16), "dp").astype(jnp.float32),
     )
     return (

time: 421 us -> 453 us (1.076)
  the two profiles are of different devices: /device:TPU:1 before, /device:TPU:2 now
where the time goes in v1:
time: 453 us; the launch traced here: 445 us
  waiting for transfers between devices  243 us (54%)
  other arithmetic  64 us (14%)
  local copies, waits for them, and re-layouts  57.4 us (13%)
  starting transfers between devices  33.6 us (7%)
  matrix products  32.8 us (7%)
  between operations  14.4 us (3%)
    all_to_all x1, waiting for transfers between devices, shards(): lax.all_to_all(out_rows.reshape(experts, slot_rows, model_width), 'expert...  60.8 us
    all_to_all x1, waiting for transfers between devices, shards(): lax.all_to_all(send_dy, 'expert', split_axis=0, concat_axis=0, tiled=True)  60.3 us
    all_to_all x1, waiting for transfers between devices, shards(): lax.all_to_all(grad_rows.reshape(experts, slot_rows, model_width), 'exper...  58.1 us
    all_to_all x1, waiting for transfers between devices, shards(): lax.all_to_all(send_x, 'expert', split_axis=0, concat_axis=0, tiled=True)  57 us
    gather x3, other arithmetic, shards(): jnp.repeat(jnp.arange(tok_count, dtype=jnp.int32), top_count, total_repea...  30.3 us
    dot_general x4, matrix products, contract(): lax.dot_general(left, right, (((left_dim,), (right_dim,)), ((), ())), pre...  22 us
    reduce_sum x1, other arithmetic, _remake_rails(): e_now = jnp.sum(lax.all_gather(payload, ax_name), 0)  15.6 us
    all_to_all x1, starting transfers between devices, shards(): lax.all_to_all(send_x, 'expert', split_axis=0, concat_axis=0, tiled=True)  12.4 us
  transfers between devices with their start and end apart: 6, of which 5 were waited for; matrix products, arithmetic and copies ran while one was open for 19% of the time, Pallas kernels for 0%

profile of v1, /device:TPU:2, one launch (start us, length us, event | category | flops | bytes accessed | tf_op | source)
XLA Modules:
  0.0 445.0 jit_solution(7503105343783433074)
XLA Ops:
  10.9 4.5 %fusion.26 = (s32[384]{0:T(512)S(1)}, s32[384,1]{0,1:T(1,128)S(1)}) fusion(s32[]{:T(128)} %bitcast.41, s32[]{:T(128)} %bitcast.42, s32[]{:T(128)} %bitcast.43, s32[]{:T(128)} %bitcast.44, s32[]{:T(128)} %bitcast.45, s32[]{:T(128)} %bitcast.47, s32[]{:T(128)} %bitcast.46, s32[1,1,3,128]{3,2,1,0:T(4,128)S(1)} %get-tuple-element.60, ...), kind=kLoop, calls=%fused_computation.94 | loop fusion | flops 5376 | bytes 6172 | tf_op jit(solution)/shard_map/jit(_take)/gather | solution.py:54
  15.6 25.6 %select_select_fusion = s32[384]{0:T(512)S(1)} fusion(pred[384]{0:T(512)(128)(4,1)S(1)} %get-tuple-element.55, pred[384]{0:T(512)(128)(4,1)S(1)} %get-tuple-element.54, pred[384]{0:T(512)(128)(4,1)S(1)} %get-tuple-element.56, pred[384]{0:T(512)(128)(4,1)S(1)} %get-tuple-element.53, pred[384]{0:T(512)(128)(4,1)S(1)} %get-tuple-element.52, ...), kind=kLoop, calls=%fused_computation.93 | loop fusion | flops 15744 | bytes 18980 | tf_op jit(solution)/shard_map/jit(_take)/gather | solution.py:54
  43.0 10.2 %scatter_custom_fusion = bf16[576,2048]{1,0:T(8,128)(2,1)} fusion(s32[384]{0:T(512)S(1)} %fusion.27, bf16[48,2048]{1,0:T(8,128)(2,1)} %param.8, s32[1024]{0:T(1024)S(1)} %pad_clamp_fusion.1, bf16[]{:T(256)} %constant.96.clone.1), kind=kCustom, calls=%fused_computation.27 | custom fusion | bytes 2359808 | tf_op jit(solution)/shard_map/scatter | solution.py:58
  53.2 4.3 reshape.186
  57.5 12.4 %all-to-all-start = ((bf16[32,18,2048]{2,1,0:T(8,128)(2,1)}), bf16[32,18,2048]{2,1,0:T(8,128)(2,1)}, u32[]{:S(2)}, u32[]{:S(2)}) async-start(bf16[32,18,2048]{2,1,0:T(8,128)(2,1)} %reshape.186), calls=%async_computation | async-start | bytes 6291456 | tf_op jit(solution)/shard_map/all_to_all | solution.py:66
  70.1 9.6 %scatter_custom_fusion.1 = bf16[576,2048]{1,0:T(8,128)(2,1)} fusion(s32[384]{0:T(512)S(1)} %fusion.27, f32[384]{0:T(512)S(1)} %mul.52, bf16[]{:T(256)} %constant.96.clone.1, bf16[48,2048]{1,0:T(8,128)(2,1)S(1)} %copy-done.5, s32[1024]{0:T(1024)S(1)} %pad_clamp_fusion.1), kind=kCustom, calls=%fused_computation.25 | custom fusion | flops 2359296 | bytes 2562050 | tf_op jit(solution)/shard_map/scatter | solution.py:63
  79.7 4.3 reshape.190
  84.0 57.0 %all-to-all-done = bf16[32,18,2048]{2,1,0:T(8,128)(2,1)} async-done(((bf16[32,18,2048]{2,1,0:T(8,128)(2,1)}), bf16[32,18,2048]{2,1,0:T(8,128)(2,1)}, u32[]{:S(2)}, u32[]{:S(2)}) %all-to-all-start) | async-done | bytes 2359328 | tf_op jit(solution)/shard_map/all_to_all | solution.py:66
  141.0 7.4 %all-to-all-start.2 = ((bf16[32,18,2048]{2,1,0:T(8,128)(2,1)}), bf16[32,18,2048]{2,1,0:T(8,128)(2,1)}, u32[]{:S(2)}, u32[]{:S(2)}) async-start(bf16[32,18,2048]{2,1,0:T(8,128)(2,1)} %reshape.190), calls=%async_computation.2 | async-start | bytes 6291456 | tf_op jit(solution)/shard_map/all_to_all | solution.py:84
  148.6 4.3 reshape.187
  153.0 5.8 %fusion.7 = f32[576,768]{1,0:T(8,128)} fusion(bf16[576,2048]{1,0:T(8,128)(2,1)} %reshape.187, bf16[1,2048,768]{2,1,0:T(8,128)(2,1)} %param.11), kind=kOutput, calls=%fused_computation.16 | convolution fusion | flops 1811939328 | bytes 7274496 | tf_op jit(solution)/shard_map/dot_general | solution.py:24
  158.8 60.3 %all-to-all-done.2 = bf16[32,18,2048]{2,1,0:T(8,128)(2,1)} async-done(((bf16[32,18,2048]{2,1,0:T(8,128)(2,1)}), bf16[32,18,2048]{2,1,0:T(8,128)(2,1)}, u32[]{:S(2)}, u32[]{:S(2)}) %all-to-all-start.2) | async-done | bytes 2359328 | tf_op jit(solution)/shard_map/all_to_all | solution.py:84
  219.1 4.3 reshape.191
  223.5 4.6 %multiply_convert_fusion.1 = bf16[576,768]{1,0:T(8,128)(2,1)S(1)} fusion(f32[576,768]{1,0:T(8,128)} %fusion.7, bf16[576,2048]{1,0:T(8,128)(2,1)} %reshape.191, bf16[1,768,2048]{2,1,0:T(8,128)(2,1)S(1)} %copy-done), kind=kOutput, calls=%fused_computation.22 | convolution fusion | flops 1815920640 | bytes 8159232 | tf_op jit(solution)/shard_map/dot_general | solution.py:18
  233.1 4.9 %fusion.12 = bf16[576,2048]{1,0:T(8,128)(2,1)} fusion(bf16[1,768,2048]{2,1,0:T(8,128)(2,1)S(1)} %copy-done, f32[576,768]{1,0:T(8,128)} %fusion.7), kind=kOutput, calls=%fused_computation.20 | convolution fusion | flops 1815330816 | bytes 7274496 | tf_op jit(solution)/shard_map/dot_general | solution.py:26
  242.2 7.7 %all-to-all-start.1 = ((bf16[32,18,2048]{2,1,0:T(8,128)(2,1)}), bf16[32,18,2048]{2,1,0:T(8,128)(2,1)S(1)}, u32[]{:S(2)}, u32[]{:S(2)}) async-start(bf16[32,18,2048]{2,1,0:T(8,128)(2,1)} %reshape.188), calls=%async_computation.1 | async-start | bytes 6291456 | tf_op jit(solution)/shard_map/all_to_all | solution.py:71
  249.9 6.8 %fusion.9 = bf16[576,2048]{1,0:T(8,128)(2,1)} fusion(bf16[576,768]{1,0:T(8,128)(2,1)} %copy-done.7, bf16[1,2048,768]{2,1,0:T(8,128)(2,1)} %param.11), kind=kOutput, calls=%fused_computation.19 | convolution fusion | flops 1813118976 | bytes 6389760 | tf_op jit(solution)/shard_map/dot_general | solution.py:18
  256.7 4.3 reshape.192
  261.0 60.8 %all-to-all-done.1 = bf16[32,18,2048]{2,1,0:T(8,128)(2,1)S(1)} async-done(((bf16[32,18,2048]{2,1,0:T(8,128)(2,1)}), bf16[32,18,2048]{2,1,0:T(8,128)(2,1)S(1)}, u32[]{:S(2)}, u32[]{:S(2)}) %all-to-all-start.1) | async-done | bytes 2359328 | tf_op jit(solution)/shard_map/all_to_all | solution.py:71
  323.5 5.6 %all-to-all-start.3 = ((bf16[32,18,2048]{2,1,0:T(8,128)(2,1)}), bf16[32,18,2048]{2,1,0:T(8,128)(2,1)}, u32[]{:S(2)}, u32[]{:S(2)}) async-start(bf16[32,18,2048]{2,1,0:T(8,128)(2,1)} %reshape.192), calls=%async_computation.3 | async-start | bytes 6291456 | tf_op jit(solution)/shard_map/all_to_all | solution.py:89
  329.4 6.6 %fusion.15 = bf16[1,768,2048]{2,1,0:T(8,128)(2,1)} fusion(bf16[576,2048]{1,0:T(8,128)(2,1)} %reshape.191, f32[576,768]{1,0:T(8,128)} %fusion.7), kind=kOutput, calls=%fused_computation.21 | convolution fusion | flops 1815724032 | bytes 7274496 | tf_op jit(solution)/shard_map/dot_general | solution.py:18
  342.2 58.1 %all-to-all-done.3 = bf16[32,18,2048]{2,1,0:T(8,128)(2,1)} async-done(((bf16[32,18,2048]{2,1,0:T(8,128)(2,1)}), bf16[32,18,2048]{2,1,0:T(8,128)(2,1)}, u32[]{:S(2)}, u32[]{:S(2)}) %all-to-all-start.3) | async-done | bytes 2359328 | tf_op jit(solution)/shard_map/all_to_all | solution.py:89
  411.8 15.6 %reduce_sum.55 = bf16[2048,768]{1,0:T(8,128)(2,1)} reduce(bf16[8,2048,768]{2,1,0:T(8,128)(2,1)} %bitcast.95, bf16[]{:T(256)} %constant.96.clone.1), dimensions={0}, to_apply=%region_7.8 | reduce | flops 11010048 | bytes 28311554 | tf_op jit(solution)/shard_map/reduce_sum | solution.py:8
  427.4 6.4 %all-reduce.2.cloned.1.call-done = bf16[1,768,2048]{2,1,0:T(8,128)(2,1)} async-done(((bf16[1,768,2048]{2,1,0:T(8,128)(2,1)}), bf16[1,768,2048]{2,1,0:T(8,128)(2,1)}) %all-reduce.2.cloned.1.call-update) | async-done | bytes 3145744 | tf_op jit(solution)/shard_map/psum | solution.py:102
  (52 shorter events, 39.0 us)
Async XLA Ops:
  7.2 216.3 %copy-start = (bf16[1,768,2048]{2,1,0:T(8,128)(2,1)S(1)}, bf16[1,768,2048]{2,1,0:T(8,128)(2,1)}, u32[]{:S(2)}) copy-start(bf16[1,768,2048]{2,1,0:T(8,128)(2,1)} %param.12) | copy-start | bytes 9437188
  57.5 12.4 %copy-start.6 = (f32[48,8]{0,1:T(8,128)S(1)}, f32[48,8]{0,1:T(8,128)}, u32[]{:S(2)}) copy-start(f32[48,8]{0,1:T(8,128)} %param.10) | copy-start | bytes 4612
  57.5 12.6 %copy-start.5 = (bf16[48,2048]{1,0:T(8,128)(2,1)S(1)}, bf16[48,2048]{1,0:T(8,128)(2,1)}, u32[]{:S(2)}) copy-start(bf16[48,2048]{1,0:T(8,128)(2,1)} %param.13) | copy-start | bytes 589828
  57.5 83.6 %all-to-all-start = ((bf16[32,18,2048]{2,1,0:T(8,128)(2,1)}), bf16[32,18,2048]{2,1,0:T(8,128)(2,1)}, u32[]{:S(2)}, u32[]{:S(2)}) async-start(bf16[32,18,2048]{2,1,0:T(8,128)(2,1)} %reshape.186), calls=%async_computation | async-start | bytes 6291456 | tf_op jit(solution)/shard_map/all_to_all | solution.py:66
  141.0 78.1 %all-to-all-start.2 = ((bf16[32,18,2048]{2,1,0:T(8,128)(2,1)}), bf16[32,18,2048]{2,1,0:T(8,128)(2,1)}, u32[]{:S(2)}, u32[]{:S(2)}) async-start(bf16[32,18,2048]{2,1,0:T(8,128)(2,1)} %reshape.190), calls=%async_computation.2 | async-start | bytes 6291456 | tf_op jit(solution)/shard_map/all_to_all | solution.py:84
  148.4 263.4 %all-gather.3.cloned.1.call-start = ((), (), s32[]{:S(2)}) async-start(), calls=%async_computation.5 | async-start | bytes 28311552 | tf_op jit(solution)/shard_map/all_gather | solution.py:8
  223.5 5.6 %copy-start.4 = (bf16[576,2048]{1,0:T(8,128)(2,1)S(1)}, bf16[576,2048]{1,0:T(8,128)(2,1)}, u32[]{:S(2)}) copy-start(bf16[576,2048]{1,0:T(8,128)(2,1)} %reshape.187) | copy-start | bytes 7077892
  228.1 0.9 copy-start.7
  242.2 79.6 %all-to-all-start.1 = ((bf16[32,18,2048]{2,1,0:T(8,128)(2,1)}), bf16[32,18,2048]{2,1,0:T(8,128)(2,1)S(1)}, u32[]{:S(2)}, u32[]{:S(2)}) async-start(bf16[32,18,2048]{2,1,0:T(8,128)(2,1)} %reshape.188), calls=%async_computation.1 | async-start | bytes 6291456 | tf_op jit(solution)/shard_map/all_to_all | solution.py:71
  321.8 1.7 copy-start.2
  323.5 76.8 %all-to-all-start.3 = ((bf16[32,18,2048]{2,1,0:T(8,128)(2,1)}), bf16[32,18,2048]{2,1,0:T(8,128)(2,1)}, u32[]{:S(2)}, u32[]{:S(2)}) async-start(bf16[32,18,2048]{2,1,0:T(8,128)(2,1)} %reshape.192), calls=%async_computation.3 | async-start | bytes 6291456 | tf_op jit(solution)/shard_map/all_to_all | solution.py:89
  329.1 104.7 %all-reduce.2.cloned.1.call-start = ((), (), s32[]{:S(2)}) async-start(), calls=%async_computation.4 | async-start | bytes 6291456 | tf_op jit(solution)/shard_map/psum | solution.py:102
  406.4 3.3 copy-start.3
  433.8 4.1 copy-start.1
Sparse Core Ops, SparseCore 0:
  233.2 121.8 all-gather.2
  357.4 76.2 all-reduce.1
